TPU v7x, 32 devices: a whole 2x2x4 slice. The times are simulated.
32 devices in a mesh: groups: 2 (over y), leaf: 4 (over z), sub: 4 (over x, core), pair: 1.
Axes of the slice: x: 2, y: 2, z: 4, core: 2. Of those that a mesh axis runs over, the one named last changes fastest.
Arguments:
- points: float32 [16, 65536], P(None, ('groups', 'leaf', 'sub')), parts along dimension 1, may hold values from -3 to 3
- vectors: float32 [32, 65536], P(None, ('groups', 'leaf', 'sub')), parts along dimension 1, may hold values from -6 to 6
- basis: float32 [64, 64, 1024], P(('groups', 'leaf', 'sub')), parts along dimension 0, may hold values from -0.1875 to 0.1875
- transfer: float32 [64, 64, 64], P(('groups', 'leaf', 'sub')), parts along dimension 0, may hold values from -0.75 to 0.75
- skeleton: float32 [64, 16, 64], P(('groups', 'leaf', 'sub')), parts along dimension 0, may hold values from -3 to 3
- parent_skel: float32 [8, 16, 64], P('groups'), parts along dimension 0, may hold values from -3 to 3
- near_list: int32 [64, 6], P(('groups', 'leaf')), parts along dimension 0, may hold values from 0 to 31, as said below
- near_count: int32 [64], P(('groups', 'leaf')), parts along dimension 0, may hold values from 1 to 6, as said below
- far_list: int32 [64, 8], P(('groups', 'leaf', 'sub')), parts along dimension 0, may hold values from 0 to 31, as said below
- parent_far: int32 [8, 3], P(('groups', 'leaf')), parts along dimension 0, may hold values from 0 to 3, as said below
Outputs:
- product: float32 [32, 65536], P(None, ('groups', 'leaf', 'sub')), parts along dimension 1
There are 2 independent parts, one for each index of `groups`. A program takes and returns all parts, laid end to end along the dimension named above; each array names one. Nothing has to cross between parts.
Inputs may be any that keep to these rules, and one draw needn't show every extreme that they name: `near_list`: row i begins with i itself, followed by distinct other leaves of the same subtree (the 8 consecutive leaves holding i); only its first near_count[i] entries are used. `near_count`: every subtree has a leaf whose count is exactly 6. `far_list`: each row holds distinct leaves outside the row's own subtree. `parent_far`: each row holds distinct subtrees other than the row's own.
All inputs are finite; a program needn't handle non-finite values.
Results may differ from a plain program's by a relative error of at most 0.0001.
Values sent between devices are 32-bit elements; how exact they have to be, the bound alone decides.
No kernel may reach another device: no remote copies, remote signals or barrier semaphores. Data moves between devices by JAX's collectives and lax.ppermute only.
A program may use at most 64 MiB of HBM per device.

v0:
```python
import functools
import math

import jax
import jax.numpy as jnp
from jax import lax
from jax.experimental import pallas as pl
from jax.experimental.pallas import tpu as pltpu
from jax.sharding import PartitionSpec as P

RATE = 0.125 * math.log2(math.e)
STRIP = 256
F32, BF16 = jnp.float32, jnp.bfloat16
VMEM = pl.BlockSpec(memory_space=pltpu.VMEM)
SMEM = pl.BlockSpec(memory_space=pltpu.SMEM)
PARAMS = pltpu.CompilerParams(vmem_limit_bytes=40 * 1024 * 1024)
NN, NT = (((1,), (0,)), ((), ())), (((1,), (1,)), ((), ()))


def mxu(x, y, dims=NN):
    return lax.dot_general(x, y, dims, preferred_element_type=F32)


def split2(x):
    high = x.astype(BF16)
    return high, (x - high.astype(F32)).astype(BF16)


def split3(x):
    high = x.astype(BF16).astype(F32)
    rest = x - high
    middle = rest.astype(BF16).astype(F32)
    return high, middle, (rest - middle).astype(BF16).astype(F32)


def product(x, y, dims=NN):
    x1, x2 = split2(x)
    y1, y2 = split2(y)
    return mxu(x1, y1, dims) + (mxu(x2, y1, dims) + mxu(x1, y2, dims))


def source_rows(x):
    a1, a2, a3 = split3(x * (2.0 * RATE))
    return jnp.concatenate([a1, a1, a2, a2, a1, a3], axis=0).T.astype(BF16)


def target_columns(x):
    b1, b2, b3 = split3(x)
    return jnp.concatenate([b1, b2, b1, b2, b3, b1], axis=0).astype(BF16)


def damping(x):
    return jnp.exp2(-RATE * jnp.sum(x * x, axis=0, keepdims=True))


def coef_kernel(leaves, vectors, basis, transfer, skeleton, packed):
    dim, rank = skeleton.shape[1:]
    width = basis.shape[2]
    vecs = vectors.shape[0]
    lift = 0.0
    for leaf in range(leaves):
        lanes = pl.ds(leaf * rank, rank)
        coef = product(vectors[:, leaf * width : (leaf + 1) * width], basis[leaf], NT)
        packed[0:dim, lanes] = skeleton[leaf]
        packed[dim : dim + vecs, lanes] = coef
        lift = lift + product(coef, transfer[leaf])
    rows = vecs // leaves
    for piece in range(leaves):
        packed[dim + vecs :, pl.ds(piece * rank, rank)] = lift[piece * rows : (piece + 1) * rows]


def coefficients(vectors, basis, transfer, skeleton):
    leaves, dim, rank = skeleton.shape
    vecs = vectors.shape[0]
    return pl.pallas_call(
        functools.partial(coef_kernel, leaves),
        out_shape=jax.ShapeDtypeStruct((dim + vecs + vecs // leaves, leaves * rank), F32),
        in_specs=[VMEM] * 4,
        out_specs=VMEM,
        compiler_params=PARAMS,
        name="coefficients",
    )(vectors, basis, transfer, skeleton)


def near_kernel(config, near_list, near_count, points, vectors, *refs):
    source_xor, target_xors, leaves, sources, width, has_start = config
    count = len(target_xors)
    targets, refs = refs[:count], refs[count:]
    starts, refs = (refs[:count], refs[count:]) if has_start else (None, refs)
    outs, (work, left, coefs, right, totals) = refs[:count], refs[count:]
    vecs = vectors.shape[0]
    group = near_list.shape[0]
    first = lax.axis_index("leaf") * group
    me = lax.axis_index("sub")
    source_base = 0 if source_xor is None else (me ^ source_xor) * leaves
    pair_size, pair_at = lax.axis_size("pair"), lax.axis_index("pair")

    todo = jnp.int32(0)
    for index, target_xor in enumerate(target_xors):
        for leaf in range(leaves):
            place = (me ^ target_xor) * leaves + leaf
            limit = near_count[place]
            for turn in range(near_list.shape[1]):
                source = near_list[place, turn] - first - source_base
                wanted = (turn < limit) & (source >= 0) & (source < sources)
                if pair_size > 1:
                    wanted = wanted & (pair_at == turn % pair_size)
                work[todo] = (index * leaves + leaf) * sources + source
                todo = todo + wanted.astype(jnp.int32)

    for source in range(sources):
        span = slice(source * width, (source + 1) * width)
        here = points[:, span]
        left[source] = source_rows(here)
        high, low = split2(vectors[:, span] * damping(here))
        coefs[source, 0:vecs] = high
        coefs[source, vecs:] = low
    for index in range(count):
        for leaf in range(leaves):
            slot = index * leaves + leaf
            right[slot] = target_columns(targets[index][:, leaf * width : (leaf + 1) * width])
            totals[slot] = jnp.zeros((vecs, width), F32)

    def tile(step, carry):
        slot = work[step] // sources
        source = work[step] % sources
        rows = left[source]
        both = coefs[source]
        for offset in range(0, width, STRIP):
            kernel = jnp.exp2(mxu(rows, right[slot, :, offset : offset + STRIP]))
            high, low = split2(kernel)
            top = mxu(both, high)
            found = top[:vecs] + (top[vecs:] + mxu(both[:vecs], low))
            totals[slot, :, offset : offset + STRIP] += found
        return carry

    lax.fori_loop(0, todo, tile, 0)
    for index in range(count):
        for leaf in range(leaves):
            span = slice(leaf * width, (leaf + 1) * width)
            scale = damping(targets[index][:, span]) * width**-0.5
            found = totals[index * leaves + leaf] * scale
            if has_start:
                found = found + starts[index][:, span]
            outs[index][:, span] = found


def near_field(lists, source, targets, source_xor, target_xors, leaves, starts=()):
    points, vectors = source
    near_list, near_count = lists
    dim, vecs = points.shape[0], vectors.shape[0]
    width = targets[0].shape[1] // leaves
    sources = points.shape[1] // width
    count = len(target_xors)
    slots = count * leaves
    config = (source_xor, target_xors, leaves, sources, width, bool(starts))
    return pl.pallas_call(
        functools.partial(near_kernel, config),
        out_shape=[jax.ShapeDtypeStruct((vecs, leaves * width), F32)] * count,
        in_specs=[SMEM, SMEM] + [VMEM] * (2 + count + len(starts)),
        out_specs=[VMEM] * count,
        scratch_shapes=[
            pltpu.SMEM((slots * near_list.shape[1] + 1,), jnp.int32),
            pltpu.VMEM((sources, width, 6 * dim), BF16),
            pltpu.VMEM((sources, 2 * vecs, width), BF16),
            pltpu.VMEM((slots, 6 * dim, width), BF16),
            pltpu.VMEM((slots, vecs, width), F32),
        ],
        compiler_params=PARAMS,
        name="near_field",
    )(near_list, near_count, points, vectors, *targets, *starts)


def interact(source, coefs, target):
    kernel = jnp.exp2(mxu(source_rows(source), target_columns(target)))
    return product(coefs * damping(source), kernel) * damping(target)


def far_kernel(place_of, leaves, subs, far_list, parent_far, *refs):
    gathered, (skeleton, parent_skel, transfer, basis, out) = refs[:-5], refs[-5:]
    dim, rank = skeleton.shape[1:]
    width = basis.shape[2]
    vecs = out.shape[0]

    def block(device):
        which, index = place_of(device)
        found = gathered[0][index]
        for other in range(1, len(gathered)):
            found = jnp.where(which == other, gathered[other][index], found)
        return found

    def lanes(data, at):
        found = data[:, :rank]
        for other in range(1, leaves):
            found = jnp.where(at == other, data[:, other * rank : (other + 1) * rank], found)
        return found

    points, coefs = [], []
    for turn in range(parent_far.shape[1]):
        parent = parent_far[0, turn]
        lift = block(parent * subs)[dim + vecs :]
        for sub in range(1, subs):
            lift = lift + block(parent * subs + sub)[dim + vecs :]
        coefs.append(
            jnp.concatenate([lift[:, at * rank : (at + 1) * rank] for at in range(leaves)], axis=0)
        )
        points.append(parent_skel[parent])
    own = parent_skel[lax.axis_index("leaf")]
    upper = interact(
        jnp.concatenate(points, axis=1), jnp.concatenate(coefs, axis=1), own
    ) * (rank**-0.5)

    for leaf in range(leaves):
        points, coefs = [], []
        for turn in range(far_list.shape[1]):
            partner = far_list[leaf, turn]
            data = lanes(block(partner // leaves), partner % leaves)
            points.append(data[:dim])
            coefs.append(data[dim : dim + vecs])
        far = interact(
            jnp.concatenate(points, axis=1), jnp.concatenate(coefs, axis=1), skeleton[leaf]
        ) * (rank**-0.5)
        field = far + product(upper, transfer[leaf], NT)
        out[:, leaf * width : (leaf + 1) * width] = product(field, basis[leaf])


def far_field(place_of, subs, far_list, parent_far, gathered, skeleton, parent_skel, transfer, basis):
    leaves, rank, width = basis.shape
    vecs = gathered[0].shape[1] - skeleton.shape[1]
    vecs = vecs * leaves // (leaves + 1)
    return pl.pallas_call(
        functools.partial(far_kernel, place_of, leaves, subs),
        out_shape=jax.ShapeDtypeStruct((vecs, leaves * width), F32),
        in_specs=[SMEM, SMEM] + [VMEM] * (len(gathered) + 4),
        out_specs=VMEM,
        compiler_params=PARAMS,
        name="far_field",
    )(far_list, parent_far, *gathered, skeleton, parent_skel, transfer, basis)


def swap(x, bit):
    size = lax.axis_size("sub")
    return lax.ppermute(x, "sub", [(at, at ^ bit) for at in range(size)])


def local(
    points,
    vectors,
    basis,
    transfer,
    skeleton,
    parent_skel,
    near_list,
    near_count,
    far_list,
    parent_far,
):
    leaves = basis.shape[0]
    subs, groups = lax.axis_size("sub"), lax.axis_size("leaf")
    lists = (near_list, near_count)
    own = (points, vectors)
    packed = coefficients(vectors, basis, transfer, skeleton)
    if subs == 4 and lax.axis_size("pair") == 1:
        cross = (swap(points, 2), swap(vectors, 2))
        twin_points = swap(points, 1)
        targets = (twin_points, points)
        line = [packed] + [
            lax.ppermute(packed, "leaf", [(at, (at + step) % groups) for at in range(groups)])
            for step in range(1, groups)
        ]
        first = near_field(lists, own, targets, 0, (1, 0), leaves)
        line = jnp.stack(line)
        plane = jnp.concatenate([line, swap(line, 2)])
        gathered = (plane, swap(plane, 1))
        (twin_near,) = near_field(lists, cross, (twin_points,), 2, (1,), leaves, (first[0],))
        back = swap(twin_near, 1)
        (near,) = near_field(lists, cross, (points,), 2, (0,), leaves, (first[1],))

        def place_of(device):
            away = (device % subs) ^ lax.axis_index("sub")
            step = (lax.axis_index("leaf") - device // subs + groups) % groups
            return away % 2, (away // 2) * groups + step

        near = near + back
    else:
        gathered = (lax.all_gather(packed, ("leaf", "sub")),)
        everyone = tuple(lax.all_gather(x, "sub", axis=1, tiled=True) for x in own)
        (near,) = near_field(lists, everyone, (points,), None, (0,), leaves)
        near = lax.psum(near, "pair")

        def place_of(device):
            return 0, device

    far = far_field(
        place_of, subs, far_list, parent_far, gathered, skeleton, parent_skel, transfer, basis
    )
    return near + far


def solution(mesh):
    placed = (
        P(None, ("groups", "leaf", "sub")),
        P(None, ("groups", "leaf", "sub")),
        P(("groups", "leaf", "sub"), None, None),
        P(("groups", "leaf", "sub"), None, None),
        P(("groups", "leaf", "sub"), None, None),
        P("groups", None, None),
        P(("groups", "leaf"), None),
        P(("groups", "leaf")),
        P(("groups", "leaf", "sub"), None),
        P(("groups", "leaf"), None),
    )
    return jax.shard_map(
        local,
        mesh=mesh,
        in_specs=placed,
        out_specs=P(None, ("groups", "leaf", "sub")),
        check_vma=False,
    )
```

profile of v0, /device:TPU:13, one launch (start us, length us, event | category | flops | bytes accessed | tf_op | source)
XLA Modules:
  0.0 39.3 jit_solution(17753033619515284239)
XLA Ops:
  0.0 1.0 %copy-done = f32[2,64,1024]{2,1,0:T(8,128)S(1)} copy-done((f32[2,64,1024]{2,1,0:T(8,128)S(1)}, f32[2,64,1024]{2,1,0:T(8,128)}, u32[]{:S(2)}) %copy-start) | copy-done | bytes 524312
  1.0 0.9 %copy-done.3 = f32[32,2048]{1,0:T(8,128)S(1)} copy-done((f32[32,2048]{1,0:T(8,128)S(1)}, f32[32,2048]{1,0:T(8,128)}, u32[]{:S(2)}) %copy-start.3) | copy-done | bytes 262168
  2.0 0.8 %copy-done.4 = f32[2,64,64]{2,1,0:T(8,128)S(1)} copy-done((f32[2,64,64]{2,1,0:T(8,128)S(1)}, f32[2,64,64]{2,1,0:T(8,128)}, u32[]{:S(2)}) %copy-start.4) | copy-done | bytes 32792
  2.8 0.7 %copy-done.6 = f32[2,16,64]{2,1,0:T(8,128)S(1)} copy-done((f32[2,16,64]{2,1,0:T(8,128)S(1)}, f32[2,16,64]{2,1,0:T(8,128)}, u32[]{:S(2)}) %copy-start.6) | copy-done | bytes 8216
  3.6 0.8 %coefficients.1 = f32[64,128]{1,0:T(8,128)S(1)} custom-call(f32[32,2048]{1,0:T(8,128)S(1)} %copy-done.3, f32[2,64,1024]{2,1,0:T(8,128)S(1)} %copy-done, f32[2,64,64]{2,1,0:T(8,128)S(1)} %copy-done.4, f32[2,16,64]{2,1,0:T(8,128)S(1)} %copy-done.6), custom_call_target="tpu_custom_call" | custom-call | tf_op jit(solution)/shard_map/coefficients/pallas_call | solution.py:75
  4.4 0.2 collective-permute-start.6
  4.6 2.3 %collective-permute-start.5 = (f32[64,128]{1,0:T(8,128)S(1)}, f32[64,128]{1,0:T(8,128)S(1)}, u32[]{:S(2)}, u32[]{:S(2)}) collective-permute-start(f32[64,128]{1,0:T(8,128)S(1)} %coefficients.1), channel_id=1, source_target_pairs={{0,8},{4,12},{8,0},{12,4},{1,9},{5,13},{9,1},{13,5},{2,10},{6,14},... | collective-permute-start | bytes 98312 | tf_op jit(solution)/shard_map/ppermute | solution.py:268
  6.9 2.2 %collective-permute-start.4 = (f32[64,128]{1,0:T(8,128)S(1)}, f32[64,128]{1,0:T(8,128)S(1)}, u32[]{:S(2)}, u32[]{:S(2)}) collective-permute-start(f32[64,128]{1,0:T(8,128)S(1)} %coefficients.1), channel_id=1, source_target_pairs={{0,4},{4,8},{8,12},{12,0},{1,5},{5,9},{9,13},{13,1},{2,6},{6,10},{... | collective-permute-start | bytes 98312 | tf_op jit(solution)/shard_map/ppermute | solution.py:268
  9.1 1.5 %collective-permute-start.2 = (f32[16,2048]{1,0:T(8,128)S(1)}, f32[16,2048]{1,0:T(8,128)S(1)}, u32[]{:S(2)}, u32[]{:S(2)}) collective-permute-start(f32[16,2048]{1,0:T(8,128)S(1)} %copy-done.2), channel_id=1, source_target_pairs={{0,1},{1,0},{2,3},{3,2},{4,5},{5,4},{6,7},{7,6},{8,9},{9,8},{10,11... | collective-permute-start | bytes 393224 | tf_op jit(solution)/shard_map/ppermute | solution.py:243
  10.6 1.2 %collective-permute-start = (f32[16,2048]{1,0:T(8,128)S(1)}, f32[16,2048]{1,0:T(8,128)S(1)}, u32[]{:S(2)}, u32[]{:S(2)}) collective-permute-start(f32[16,2048]{1,0:T(8,128)S(1)} %copy-done.2), channel_id=1, source_target_pairs={{0,2},{1,3},{2,0},{3,1},{4,6},{5,7},{6,4},{7,5},{8,10},{9,11},{10,... | collective-permute-start | bytes 393224 | tf_op jit(solution)/shard_map/ppermute | solution.py:243
  11.8 0.0 collective-permute-done.6
  11.8 0.3 collective-permute-start.1
  12.1 0.0 collective-permute-done.5
  12.1 0.0 collective-permute-done.4
  12.1 1.3 %collective-permute-start.7 = (f32[4,64,128]{2,1,0:T(8,128)S(1)}, f32[4,64,128]{2,1,0:T(8,128)S(1)}, u32[]{:S(2)}, u32[]{:S(2)}) collective-permute-start(f32[4,64,128]{2,1,0:T(8,128)S(1)} %pad_maximum_fusion), channel_id=1, source_target_pairs={{0,2},{1,3},{2,0},{3,1},{4,6},{5,7},{6,4},{7,5},{8,10},{9,11},{10,... | collective-permute-start | bytes 393224 | tf_op jit(solution)/shard_map/ppermute | solution.py:243
  13.4 0.0 copy-start.8
  13.4 0.0 copy-start.10
  13.4 0.6 %copy-done.8 = s32[8,6]{1,0:T(8,128)S(1)} copy-done((s32[8,6]{1,0:T(8,128)S(1)}, s32[8,6]{1,0:T(8,128)}, u32[]{:S(2)}) %copy-start.8) | copy-done | bytes 216
  14.1 4.1 %near_field.3 = (f32[32,2048]{1,0:T(8,128)S(1)}, f32[32,2048]{1,0:T(8,128)S(1)}) custom-call(s32[8,6]{1,0:T(8,128)S(1)} %copy-done.8, s32[8]{0:T(128)S(1)} %copy-done.10, f32[16,2048]{1,0:T(8,128)S(1)} %copy-done.2, f32[32,2048]{1,0:T(8,128)S(1)} %copy-done.3, f32[16,2048]{1,0:T(8,128)S(1)} %collective-permute-done.2.refs_0_, f32[16,2048]{1,0:T(8,128)S(1)} %copy-done.2), custom_call_target="tpu_custom_call" | custom-call | tf_op jit(solution)/shard_map/near_field/pallas_call | solution.py:157
  18.2 6.0 %collective-permute-done.7 = f32[4,64,128]{2,1,0:T(8,128)S(1)} collective-permute-done((f32[4,64,128]{2,1,0:T(8,128)S(1)}, f32[4,64,128]{2,1,0:T(8,128)S(1)}, u32[]{:S(2)}, u32[]{:S(2)}) %collective-permute-start.7) | collective-permute-done | bytes 131104 | tf_op jit(solution)/shard_map/ppermute | solution.py:243
  24.2 0.8 %collective-permute-start.8 = (f32[8,64,128]{2,1,0:T(8,128)S(1)}, f32[8,64,128]{2,1,0:T(8,128)S(1)}, u32[]{:S(2)}, u32[]{:S(2)}) collective-permute-start(f32[8,64,128]{2,1,0:T(8,128)S(1)} %constant_dynamic-update-slice_fusion.refs_0_), channel_id=1, source_target_pairs={{0,1},{1,0},{2,3},{3,2},{4,5},{5,4},{6,7},{7,6},{8,9},{9,8},{10,11... | collective-permute-start | bytes 786440 | tf_op jit(solution)/shard_map/ppermute | solution.py:243
  25.0 4.0 %near_field.5 = f32[32,2048]{1,0:T(8,128)S(1)} custom-call(s32[8,6]{1,0:T(8,128)S(1)} %copy-done.8, s32[8]{0:T(128)S(1)} %copy-done.10, f32[16,2048]{1,0:T(8,128)S(1)} %collective-permute-done.points, f32[32,2048]{1,0:T(8,128)S(1)} %collective-permute-done.1.vectors, f32[16,2048]{1,0:T(8,128)S(1)} %collective-permute-done.2.refs_0_, ...), custom_call_target="tpu_custom_call" | custom-call | tf_op jit(solution)/shard_map/near_field/pallas_call | solution.py:157
  29.1 0.1 collective-permute-start.3
  29.2 0.0 copy-start.7
  29.2 0.0 copy-start.9
  29.2 0.0 copy-start.11
  29.2 0.0 copy-start.12
  29.2 7.2 %near_field.4 = f32[32,2048]{1,0:T(8,128)S(1)} custom-call(s32[8,6]{1,0:T(8,128)S(1)} %copy-done.8, s32[8]{0:T(128)S(1)} %copy-done.10, f32[16,2048]{1,0:T(8,128)S(1)} %collective-permute-done.points, f32[32,2048]{1,0:T(8,128)S(1)} %collective-permute-done.1.vectors, f32[16,2048]{1,0:T(8,128)S(1)} %copy-done.2, f32[32,2048]{1,0:T(8,128)S(1)} %get-tuple-element.7.refs_1_), custom_call_target="tpu_custom_call" | custom-call | tf_op jit(solution)/shard_map/near_field/pallas_call | solution.py:157
  36.4 0.0 collective-permute-done.8.refs_1_
  36.4 2.1 %far_field.1 = f32[32,2048]{1,0:T(8,128)S(1)} custom-call(s32[2,8]{1,0:T(2,128)S(1)} %copy-done.11, s32[1,3]{1,0:T(1,128)S(1)} %copy-done.12, f32[8,64,128]{2,1,0:T(8,128)S(1)} %constant_dynamic-update-slice_fusion.refs_0_, f32[8,64,128]{2,1,0:T(8,128)S(1)} %collective-permute-done.8.refs_1_, f32[2,16,64]{2,1,0:T(8,128)S(1)} %copy-done.7, ...), custom_call_target="tpu_custom_call" | custom-call | tf_op jit(solution)/shard_map/far_field/pallas_call | solution.py:231
  38.6 0.0 collective-permute-done.3
  38.6 0.8 %add_add_fusion = f32[32,2048]{1,0:T(8,128)} fusion(f32[32,2048]{1,0:T(8,128)S(1)} %far_field.1, f32[32,2048]{1,0:T(8,128)S(1)} %near_field.4, f32[32,2048]{1,0:T(8,128)S(1)} %collective-permute-done.3), kind=kLoop, calls=%fused_computation | loop fusion | flops 131072 | bytes 1048576 | tf_op jit(solution)/shard_map/add | solution.py:297
  (24 shorter events, 0.1 us)
Async XLA Ops:
  0.0 1.0 %copy-start = (f32[2,64,1024]{2,1,0:T(8,128)S(1)}, f32[2,64,1024]{2,1,0:T(8,128)}, u32[]{:S(2)}) copy-start(f32[2,64,1024]{2,1,0:T(8,128)} %refs_5_.1) | copy-start | bytes 1572868
  1.0 0.9 %copy-start.3 = (f32[32,2048]{1,0:T(8,128)S(1)}, f32[32,2048]{1,0:T(8,128)}, u32[]{:S(2)}) copy-start(f32[32,2048]{1,0:T(8,128)} %vectors.3) | copy-start | bytes 786436
  2.0 0.8 %copy-start.4 = (f32[2,64,64]{2,1,0:T(8,128)S(1)}, f32[2,64,64]{2,1,0:T(8,128)}, u32[]{:S(2)}) copy-start(f32[2,64,64]{2,1,0:T(8,128)} %refs_4_.1) | copy-start | bytes 98308
  2.8 0.7 %copy-start.6 = (f32[2,16,64]{2,1,0:T(8,128)S(1)}, f32[2,16,64]{2,1,0:T(8,128)}, u32[]{:S(2)}) copy-start(f32[2,16,64]{2,1,0:T(8,128)} %refs_2_.1) | copy-start | bytes 24580
  3.6 5.5 %copy-start.2 = (f32[16,2048]{1,0:T(8,128)S(1)}, f32[16,2048]{1,0:T(8,128)}, u32[]{:S(2)}) copy-start(f32[16,2048]{1,0:T(8,128)} %refs_0_.1) | copy-start | bytes 393220
  4.4 7.4 %collective-permute-start.6 = (f32[64,128]{1,0:T(8,128)S(1)}, f32[64,128]{1,0:T(8,128)S(1)}, u32[]{:S(2)}, u32[]{:S(2)}) collective-permute-start(f32[64,128]{1,0:T(8,128)S(1)} %coefficients.1), channel_id=1, source_target_pairs={{0,12},{4,0},{8,4},{12,8},{1,13},{5,1},{9,5},{13,9},{2,14},{6,2},{... | collective-permute-start | bytes 98312 | tf_op jit(solution)/shard_map/ppermute | solution.py:268
  4.6 7.5 %collective-permute-start.5 = (f32[64,128]{1,0:T(8,128)S(1)}, f32[64,128]{1,0:T(8,128)S(1)}, u32[]{:S(2)}, u32[]{:S(2)}) collective-permute-start(f32[64,128]{1,0:T(8,128)S(1)} %coefficients.1), channel_id=1, source_target_pairs={{0,8},{4,12},{8,0},{12,4},{1,9},{5,13},{9,1},{13,5},{2,10},{6,14},... | collective-permute-start | bytes 98312 | tf_op jit(solution)/shard_map/ppermute | solution.py:268
  6.9 5.2 %collective-permute-start.4 = (f32[64,128]{1,0:T(8,128)S(1)}, f32[64,128]{1,0:T(8,128)S(1)}, u32[]{:S(2)}, u32[]{:S(2)}) collective-permute-start(f32[64,128]{1,0:T(8,128)S(1)} %coefficients.1), channel_id=1, source_target_pairs={{0,4},{4,8},{8,12},{12,0},{1,5},{5,9},{9,13},{13,1},{2,6},{6,10},{... | collective-permute-start | bytes 98312 | tf_op jit(solution)/shard_map/ppermute | solution.py:268
  9.1 4.3 %collective-permute-start.2 = (f32[16,2048]{1,0:T(8,128)S(1)}, f32[16,2048]{1,0:T(8,128)S(1)}, u32[]{:S(2)}, u32[]{:S(2)}) collective-permute-start(f32[16,2048]{1,0:T(8,128)S(1)} %copy-done.2), channel_id=1, source_target_pairs={{0,1},{1,0},{2,3},{3,2},{4,5},{5,4},{6,7},{7,6},{8,9},{9,8},{10,11... | collective-permute-start | bytes 393224 | tf_op jit(solution)/shard_map/ppermute | solution.py:243
  10.6 14.4 %collective-permute-start = (f32[16,2048]{1,0:T(8,128)S(1)}, f32[16,2048]{1,0:T(8,128)S(1)}, u32[]{:S(2)}, u32[]{:S(2)}) collective-permute-start(f32[16,2048]{1,0:T(8,128)S(1)} %copy-done.2), channel_id=1, source_target_pairs={{0,2},{1,3},{2,0},{3,1},{4,6},{5,7},{6,4},{7,5},{8,10},{9,11},{10,... | collective-permute-start | bytes 393224 | tf_op jit(solution)/shard_map/ppermute | solution.py:243
  11.8 13.2 %collective-permute-start.1 = (f32[32,2048]{1,0:T(8,128)S(1)}, f32[32,2048]{1,0:T(8,128)S(1)}, u32[]{:S(2)}, u32[]{:S(2)}) collective-permute-start(f32[32,2048]{1,0:T(8,128)S(1)} %copy-done.3), channel_id=1, source_target_pairs={{0,2},{1,3},{2,0},{3,1},{4,6},{5,7},{6,4},{7,5},{8,10},{9,11},{10,... | collective-permute-start | bytes 786440 | tf_op jit(solution)/shard_map/ppermute | solution.py:243
  12.1 12.1 %collective-permute-start.7 = (f32[4,64,128]{2,1,0:T(8,128)S(1)}, f32[4,64,128]{2,1,0:T(8,128)S(1)}, u32[]{:S(2)}, u32[]{:S(2)}) collective-permute-start(f32[4,64,128]{2,1,0:T(8,128)S(1)} %pad_maximum_fusion), channel_id=1, source_target_pairs={{0,2},{1,3},{2,0},{3,1},{4,6},{5,7},{6,4},{7,5},{8,10},{9,11},{10,... | collective-permute-start | bytes 393224 | tf_op jit(solution)/shard_map/ppermute | solution.py:243
  13.4 0.7 %copy-start.8 = (s32[8,6]{1,0:T(8,128)S(1)}, s32[8,6]{1,0:T(8,128)}, u32[]{:S(2)}) copy-start(s32[8,6]{1,0:T(8,128)} %near_list.5) | copy-start | bytes 580
  13.4 0.7 %copy-start.10 = (s32[8]{0:T(128)S(1)}, s32[8]{0:T(128)}, u32[]{:S(2)}) copy-start(s32[8]{0:T(128)} %near_count.5) | copy-start | bytes 100
  24.2 12.2 %collective-permute-start.8 = (f32[8,64,128]{2,1,0:T(8,128)S(1)}, f32[8,64,128]{2,1,0:T(8,128)S(1)}, u32[]{:S(2)}, u32[]{:S(2)}) collective-permute-start(f32[8,64,128]{2,1,0:T(8,128)S(1)} %constant_dynamic-update-slice_fusion.refs_0_), channel_id=1, source_target_pairs={{0,1},{1,0},{2,3},{3,2},{4,5},{5,4},{6,7},{7,6},{8,9},{9,8},{10,11... | collective-permute-start | bytes 786440 | tf_op jit(solution)/shard_map/ppermute | solution.py:243
  29.1 9.5 %collective-permute-start.3 = (f32[32,2048]{1,0:T(8,128)S(1)}, f32[32,2048]{1,0:T(8,128)S(1)}, u32[]{:S(2)}, u32[]{:S(2)}) collective-permute-start(f32[32,2048]{1,0:T(8,128)S(1)} %near_field.5), channel_id=1, source_target_pairs={{0,1},{1,0},{2,3},{3,2},{4,5},{5,4},{6,7},{7,6},{8,9},{9,8},{10,11... | collective-permute-start | bytes 786440 | tf_op jit(solution)/shard_map/ppermute | solution.py:243
  29.2 7.2 %copy-start.1 = (f32[2,64,1024]{2,1,0:T(8,128)S(1)}, f32[2,64,1024]{2,1,0:T(8,128)}, u32[]{:S(2)}) copy-start(f32[2,64,1024]{2,1,0:T(8,128)} %refs_5_.1) | copy-start | bytes 1572868
  29.2 7.2 %copy-start.5 = (f32[2,64,64]{2,1,0:T(8,128)S(1)}, f32[2,64,64]{2,1,0:T(8,128)}, u32[]{:S(2)}) copy-start(f32[2,64,64]{2,1,0:T(8,128)} %refs_4_.1) | copy-start | bytes 98308
  29.2 7.2 %copy-start.7 = (f32[2,16,64]{2,1,0:T(8,128)S(1)}, f32[2,16,64]{2,1,0:T(8,128)}, u32[]{:S(2)}) copy-start(f32[2,16,64]{2,1,0:T(8,128)} %refs_2_.1) | copy-start | bytes 24580
  29.2 7.2 %copy-start.9 = (f32[4,16,64]{2,1,0:T(8,128)S(1)}, f32[4,16,64]{2,1,0:T(8,128)}, u32[]{:S(2)}) copy-start(f32[4,16,64]{2,1,0:T(8,128)} %refs_3_.1) | copy-start | bytes 49156
  29.2 7.2 %copy-start.11 = (s32[2,8]{1,0:T(2,128)S(1)}, s32[2,8]{1,0:T(2,128)}, u32[]{:S(2)}) copy-start(s32[2,8]{1,0:T(2,128)} %far_list.1) | copy-start | bytes 196
  29.2 7.2 %copy-start.12 = (s32[1,3]{1,0:T(1,128)S(1)}, s32[1,3]{1,0:T(1,128)}, u32[]{:S(2)}) copy-start(s32[1,3]{1,0:T(1,128)} %parent_far.1) | copy-start | bytes 40
where the time goes:
time: 38.8 us; the launch traced here: 39.3 us
  Pallas kernels  18.3 us (47%)
  starting transfers between devices  9.89 us (25%)
  waiting for transfers between devices  5.99 us (15%)
  local copies, waits for them, and re-layouts  4.26 us (11%)
  other arithmetic  0.77 us (2%)
    pallas_call x3, Pallas kernels, near_field(): pl.pallas_call(functools.partial(near_kernel, config), out_shape=[jax.Sha...  15.3 us
    ppermute x6, waiting for transfers between devices, swap(): return lax.ppermute(x, 'sub', [(at, at ^ bit) for at in range(size)])  5.98 us
    ppermute x6, starting transfers between devices, swap(): return lax.ppermute(x, 'sub', [(at, at ^ bit) for at in range(size)])  5.21 us
    ppermute x3, starting transfers between devices, local(): lax.ppermute(packed, 'leaf', [(at, (at + step) % groups) for at in range(...  4.69 us
    unnamed x30, local copies, waits for them, and re-layouts  4.25 us
    pallas_call x1, Pallas kernels, far_field(): pl.pallas_call(functools.partial(far_kernel, place_of, leaves, subs), out...  2.14 us
    pallas_call x1, Pallas kernels, coefficients(): pl.pallas_call(functools.partial(coef_kernel, leaves), out_shape=jax.Shap...  0.84 us
  transfers between devices with their start and end apart: 9, of which 1 were waited for; matrix products, arithmetic and copies ran while one was open for 0% of the time, Pallas kernels for 44%

commit v1 on v0

v1 whole, which is shorter than its diff:
```python
import functools
import math

import jax
import jax.numpy as jnp
from jax import lax
from jax.experimental import pallas as pl
from jax.experimental.pallas import tpu as pltpu
from jax.sharding import PartitionSpec as P

RATE = 0.125 * math.log2(math.e)
STRIP = 256
F32, BF16 = jnp.float32, jnp.bfloat16
VMEM = pl.BlockSpec(memory_space=pltpu.VMEM)
HBM = pl.BlockSpec(memory_space=pltpu.HBM)
SMEM = pl.BlockSpec(memory_space=pltpu.SMEM)
PARAMS = pltpu.CompilerParams(vmem_limit_bytes=40 * 1024 * 1024)
NN, NT = (((1,), (0,)), ((), ())), (((1,), (1,)), ((), ()))


def lasts(microseconds):
    return pl.CostEstimate(
        flops=int(1e9 * microseconds), bytes_accessed=int(3e6 * microseconds), transcendentals=0
    )


def mxu(x, y, dims=NN):
    return lax.dot_general(x, y, dims, preferred_element_type=F32)


def split2(x):
    high = x.astype(BF16)
    return high, (x - high.astype(F32)).astype(BF16)


def split3(x):
    high = x.astype(BF16).astype(F32)
    rest = x - high
    middle = rest.astype(BF16).astype(F32)
    return high, middle, (rest - middle).astype(BF16).astype(F32)


def product(x, y, dims=NN):
    x1, x2 = split2(x)
    y1, y2 = split2(y)
    return mxu(x1, y1, dims) + (mxu(x2, y1, dims) + mxu(x1, y2, dims))


def source_rows(x):
    a1, a2, a3 = split3(x * (2.0 * RATE))
    return jnp.concatenate([a1, a1, a2, a2, a1, a3], axis=0).T.astype(BF16)


def target_columns(x):
    b1, b2, b3 = split3(x)
    return jnp.concatenate([b1, b2, b1, b2, b3, b1], axis=0).astype(BF16)


def damping(x):
    return jnp.exp2(-RATE * jnp.sum(x * x, axis=0, keepdims=True))


def prepare_kernel(leaves, points, vectors, basis, transfer, skeleton, *refs):
    packed, left, coefs, right, scale = refs[:5]
    here, held, bases, moves, skeletons, sems = refs[5:]
    pairs = [(points, here), (vectors, held), (transfer, moves), (skeleton, skeletons)]
    pairs += [(basis.at[leaf], bases.at[leaf]) for leaf in range(leaves)]
    loads = [pltpu.make_async_copy(src, dst, sems.at[at]) for at, (src, dst) in enumerate(pairs)]
    for load in loads:
        load.start()
    dim, rank = skeletons.shape[1:]
    width = bases.shape[2]
    vecs = held.shape[0]
    spans = [slice(leaf * width, (leaf + 1) * width) for leaf in range(leaves)]
    loads[0].wait()
    fade = damping(here[...])
    scale[...] = fade * width**-0.5
    for leaf, span in enumerate(spans):
        left[leaf] = source_rows(here[:, span])
        right[leaf] = target_columns(here[:, span])
    loads[1].wait()
    for leaf, span in enumerate(spans):
        high, low = split2(held[:, span] * fade[:, span])
        coefs[leaf, 0:vecs] = high
        coefs[leaf, vecs:] = low
    loads[2].wait()
    loads[3].wait()
    lift = 0.0
    for leaf, span in enumerate(spans):
        loads[4 + leaf].wait()
        lanes = slice(leaf * rank, (leaf + 1) * rank)
        coef = product(held[:, span], bases[leaf], NT)
        packed[0:dim, lanes] = skeletons[leaf]
        packed[dim : dim + vecs, lanes] = coef
        lift = lift + product(coef, moves[leaf])
    rows = vecs // leaves
    for piece in range(leaves):
        packed[dim + vecs :, piece * rank : (piece + 1) * rank] = lift[
            piece * rows : (piece + 1) * rows
        ]


def prepare(points, vectors, basis, transfer, skeleton):
    leaves, dim, rank = skeleton.shape
    vecs = vectors.shape[0]
    width = basis.shape[2]
    inputs = [
        pltpu.with_memory_space_constraint(x, pltpu.HBM)
        for x in (points, vectors, basis, transfer, skeleton)
    ]
    return pl.pallas_call(
        functools.partial(prepare_kernel, leaves),
        out_shape=[
            jax.ShapeDtypeStruct((dim + vecs + vecs // leaves, leaves * rank), F32),
            jax.ShapeDtypeStruct((leaves, width, 6 * dim), BF16),
            jax.ShapeDtypeStruct((leaves, 2 * vecs, width), BF16),
            jax.ShapeDtypeStruct((leaves, 6 * dim, width), BF16),
            jax.ShapeDtypeStruct((1, leaves * width), F32),
        ],
        in_specs=[HBM] * 5,
        out_specs=[VMEM] * 5,
        scratch_shapes=[pltpu.VMEM(x.shape, F32) for x in inputs]
        + [pltpu.SemaphoreType.DMA((4 + leaves,))],
        compiler_params=PARAMS,
        cost_estimate=lasts(0.5),
        name="prepare",
    )(*inputs)


def near_kernel(config, near_list, near_count, *refs):
    source_xor, target_xor, leaves, sources, width, fresh_source, fresh_target, begun, last = config
    refs = list(refs)
    take = lambda count: [refs.pop(0) for _ in range(count)]
    given_source, given_target = take(2), take(1 if fresh_target else 2)
    start = take(1)[0] if begun else None
    out = take(1)[0]
    left, coefs = take(2) if fresh_source else given_source
    right, scale = take(2) if fresh_target else given_target
    (work,) = take(1)
    totals = take(1)[0] if last else out
    vecs = coefs.shape[1] // 2
    group = near_list.shape[0]
    first = lax.axis_index("leaf") * group
    me = lax.axis_index("sub")
    source_base = 0 if source_xor is None else (me ^ source_xor) * leaves
    pair_size, pair_at = lax.axis_size("pair"), lax.axis_index("pair")

    todo = jnp.int32(0)
    for leaf in range(leaves):
        place = (me ^ target_xor) * leaves + leaf
        limit = near_count[place]
        for turn in range(near_list.shape[1]):
            source = near_list[place, turn] - first - source_base
            wanted = (turn < limit) & (source >= 0) & (source < sources)
            if pair_size > 1:
                wanted = wanted & (pair_at == turn % pair_size)
            work[todo] = leaf * sources + source
            todo = todo + wanted.astype(jnp.int32)

    if fresh_source:
        points, vectors = given_source
        for source in range(sources):
            span = slice(source * width, (source + 1) * width)
            here = points[:, span]
            left[source] = source_rows(here)
            high, low = split2(vectors[:, span] * damping(here))
            coefs[source, 0:vecs] = high
            coefs[source, vecs:] = low
    if fresh_target:
        here = given_target[0]
        scale[...] = damping(here[...]) * width**-0.5
        for leaf in range(leaves):
            right[leaf] = target_columns(here[:, leaf * width : (leaf + 1) * width])
    for leaf in range(leaves):
        totals[leaf] = start[leaf] if begun else jnp.zeros((vecs, width), F32)

    def tile(step, carry):
        slot = work[step] // sources
        source = work[step] % sources
        chunks = [(y, x) for y in range(0, width, STRIP) for x in range(0, width, STRIP)]

        def exponent(y, x):
            return mxu(left[source, x : x + STRIP], right[slot, :, y : y + STRIP])

        ahead = exponent(*chunks[0])
        for at, (y, x) in enumerate(chunks):
            power = ahead
            if at + 1 < len(chunks):
                ahead = exponent(*chunks[at + 1])
            high, low = split2(jnp.exp2(power))
            both = coefs[source, :, x : x + STRIP]
            top = mxu(both, high)
            found = top[:vecs] + (top[vecs:] + mxu(both[:vecs], low))
            strip = found if x == 0 else strip + found
            if x + STRIP == width:
                totals[slot, :, y : y + STRIP] += strip
        return carry

    lax.fori_loop(0, todo, tile, 0)
    if last:
        for leaf in range(leaves):
            span = slice(leaf * width, (leaf + 1) * width)
            out[:, span] = totals[leaf] * scale[:, span]


def near_field(lists, source, target, source_xor, target_xor, leaves, start=None, last=False):
    near_list, near_count = lists
    fresh_source, fresh_target = source[0].ndim == 2, len(target) == 1
    if fresh_source:
        dim, vecs = source[0].shape[0], source[1].shape[0]
    else:
        dim, vecs = source[0].shape[2] // 6, source[1].shape[1] // 2
    width = target[-1].shape[1] // leaves
    sources = source[0].shape[1] // width if fresh_source else source[0].shape[0]
    config = (
        source_xor, target_xor, leaves, sources, width, fresh_source, fresh_target,
        start is not None, last,
    )
    totals = (leaves, vecs, width)
    shapes = [jax.ShapeDtypeStruct((vecs, leaves * width) if last else totals, F32)]
    if fresh_source:
        shapes += [
            jax.ShapeDtypeStruct((sources, width, 6 * dim), BF16),
            jax.ShapeDtypeStruct((sources, 2 * vecs, width), BF16),
        ]
    if fresh_target:
        shapes += [
            jax.ShapeDtypeStruct((leaves, 6 * dim, width), BF16),
            jax.ShapeDtypeStruct((1, leaves * width), F32),
        ]
    inputs = (*source, *target) + (() if start is None else (start,))
    scratch = [pltpu.SMEM((leaves * near_list.shape[1] + 1,), jnp.int32)]
    return pl.pallas_call(
        functools.partial(near_kernel, config),
        out_shape=shapes,
        in_specs=[SMEM, SMEM] + [VMEM] * len(inputs),
        out_specs=[VMEM] * len(shapes),
        scratch_shapes=scratch + ([pltpu.VMEM(totals, F32)] if last else []),
        compiler_params=PARAMS,
        cost_estimate=lasts(0.5),
        name="near_field",
    )(near_list, near_count, *inputs)


def interact(source, coefs, target):
    kernel = jnp.exp2(mxu(source_rows(source), target_columns(target)))
    return product(coefs * damping(source), kernel) * damping(target)


def far_kernel(place_of, leaves, subs, far_list, parent_far, *refs):
    gathered, (skeleton, parent_skel, transfer, basis, out) = refs[:-5], refs[-5:]
    dim, rank = skeleton.shape[1:]
    width = basis.shape[2]
    vecs = out.shape[0]

    def block(device):
        which, *index = place_of(device)
        found = gathered[0][tuple(index)]
        for other in range(1, len(gathered)):
            found = jnp.where(which == other, gathered[other][tuple(index)], found)
        return found

    def lanes(data, at):
        found = data[:, :rank]
        for other in range(1, leaves):
            found = jnp.where(at == other, data[:, other * rank : (other + 1) * rank], found)
        return found

    points, coefs = [], []
    for turn in range(parent_far.shape[1]):
        parent = parent_far[0, turn]
        lift = block(parent * subs)[dim + vecs :]
        for sub in range(1, subs):
            lift = lift + block(parent * subs + sub)[dim + vecs :]
        coefs.append(
            jnp.concatenate([lift[:, at * rank : (at + 1) * rank] for at in range(leaves)], axis=0)
        )
        points.append(parent_skel[parent])
    own = parent_skel[lax.axis_index("leaf")]
    upper = interact(
        jnp.concatenate(points, axis=1), jnp.concatenate(coefs, axis=1), own
    ) * (rank**-0.5)

    for leaf in range(leaves):
        points, coefs = [], []
        for turn in range(far_list.shape[1]):
            partner = far_list[leaf, turn]
            data = lanes(block(partner // leaves), partner % leaves)
            points.append(data[:dim])
            coefs.append(data[dim : dim + vecs])
        far = interact(
            jnp.concatenate(points, axis=1), jnp.concatenate(coefs, axis=1), skeleton[leaf]
        ) * (rank**-0.5)
        field = far + product(upper, transfer[leaf], NT)
        out[:, leaf * width : (leaf + 1) * width] = product(field, basis[leaf])


def far_field(place_of, subs, far_list, parent_far, gathered, skeleton, parent_skel, transfer, basis):
    leaves, rank, width = basis.shape
    vecs = gathered[0].shape[-2] - skeleton.shape[1]
    vecs = vecs * leaves // (leaves + 1)
    return pl.pallas_call(
        functools.partial(far_kernel, place_of, leaves, subs),
        out_shape=jax.ShapeDtypeStruct((vecs, leaves * width), F32),
        in_specs=[SMEM, SMEM] + [VMEM] * (len(gathered) + 4),
        out_specs=VMEM,
        compiler_params=PARAMS,
        cost_estimate=lasts(0.5),
        name="far_field",
    )(far_list, parent_far, *gathered, skeleton, parent_skel, transfer, basis)


def swap(x, bit):
    size = lax.axis_size("sub")
    return lax.ppermute(x, "sub", [(at, at ^ bit) for at in range(size)])


def local(
    points,
    vectors,
    basis,
    transfer,
    skeleton,
    parent_skel,
    near_list,
    near_count,
    far_list,
    parent_far,
):
    leaves = basis.shape[0]
    subs, groups = lax.axis_size("sub"), lax.axis_size("leaf")
    lists = (near_list, near_count)
    packed, *factors = prepare(points, vectors, basis, transfer, skeleton)
    own, own_target = factors[:2], factors[2:]
    if subs == 4 and lax.axis_size("pair") == 1:
        cross_points = swap(points, 2)
        column = jnp.stack([packed, swap(packed, 2)])
        cross = (cross_points, swap(vectors, 2))
        twin = (swap(points, 1),)
        (near,) = near_field(lists, own, own_target, 0, 0, leaves)
        column, near, twin = lax.optimization_barrier((column, near, twin))
        line = [
            lax.ppermute(column, "leaf", [(at, (at + step) % groups) for at in range(groups)])
            for step in range(1, groups)
        ]
        twin_near, *twin = near_field(lists, own, twin, 0, 1, leaves)
        line, twin_near = lax.optimization_barrier((line, twin_near))
        plane = jnp.stack([column] + line)
        gathered = (plane, swap(plane, 1))
        twin_near, *cross = near_field(lists, cross, twin, 2, 1, leaves, twin_near, True)
        back = swap(twin_near, 1)
        (near,) = near_field(lists, cross, own_target, 2, 0, leaves, near, True)

        def place_of(device):
            away = (device % subs) ^ lax.axis_index("sub")
            step = (lax.axis_index("leaf") - device // subs + groups) % groups
            return away % 2, step, away // 2

        near = near + back
    else:
        gathered = (lax.all_gather(packed, ("leaf", "sub")),)
        everyone = tuple(
            lax.all_gather(x, "sub", axis=1, tiled=True) for x in (points, vectors)
        )
        near, *_ = near_field(lists, everyone, own_target, None, 0, leaves, None, True)
        near = lax.psum(near, "pair")

        def place_of(device):
            return 0, device

    far = far_field(
        place_of, subs, far_list, parent_far, gathered, skeleton, parent_skel, transfer, basis
    )
    return near + far


def solution(mesh):
    placed = (
        P(None, ("groups", "leaf", "sub")),
        P(None, ("groups", "leaf", "sub")),
        P(("groups", "leaf", "sub"), None, None),
        P(("groups", "leaf", "sub"), None, None),
        P(("groups", "leaf", "sub"), None, None),
        P("groups", None, None),
        P(("groups", "leaf"), None),
        P(("groups", "leaf")),
        P(("groups", "leaf", "sub"), None),
        P(("groups", "leaf"), None),
    )
    return jax.shard_map(
        local,
        mesh=mesh,
        in_specs=placed,
        out_specs=P(None, ("groups", "leaf", "sub")),
        check_vma=False,
    )
```

time: 38.8 us -> 35.8 us (0.923)
  the two profiles are of different devices: /device:TPU:13 before, /device:TPU:0 now
where the time goes in v1:
time: 35.8 us; the launch traced here: 36.1 us
  Pallas kernels  22 us (61%)
  starting transfers between devices  10.3 us (29%)
  waiting for transfers between devices  2.15 us (6%)
  other arithmetic  0.78 us (2%)
  local copies, waits for them, and re-layouts  0.7 us (2%)
    pallas_call x4, Pallas kernels, near_field(): pl.pallas_call(functools.partial(near_kernel, config), out_shape=shapes,...  17.6 us
    ppermute x6, starting transfers between devices, swap(): return lax.ppermute(x, 'sub', [(at, at ^ bit) for at in range(size)])  5.64 us
    ppermute x3, starting transfers between devices, local(): lax.ppermute(column, 'leaf', [(at, (at + step) % groups) for at in range(...  4.66 us
    pallas_call x1, Pallas kernels, prepare(): pl.pallas_call(functools.partial(prepare_kernel, leaves), out_shape=[jax....  2.24 us
    ppermute x3, waiting for transfers between devices, local(): lax.ppermute(column, 'leaf', [(at, (at + step) % groups) for at in range(...  2.14 us
    pallas_call x1, Pallas kernels, far_field(): pl.pallas_call(functools.partial(far_kernel, place_of, leaves, subs), out...  2.13 us
    add x1, other arithmetic, local(): return near + far  0.76 us
  transfers between devices with their start and end apart: 9, of which 1 were waited for; matrix products, arithmetic and copies ran while one was open for 0% of the time, Pallas kernels for 61%

profile of v1, /device:TPU:0, one launch (start us, length us, event | category | flops | bytes accessed | tf_op | source)
XLA Modules:
  0.0 36.1 jit_solution(4752724718609333499)
XLA Ops:
  0.0 0.5 %collective-permute-start.3 = (f32[16,2048]{1,0:T(8,128)}, f32[16,2048]{1,0:T(8,128)S(1)}, u32[]{:S(2)}, u32[]{:S(2)}) collective-permute-start(f32[16,2048]{1,0:T(8,128)} %points.1), channel_id=1, source_target_pairs={{0,1},{1,0},{2,3},{3,2},{4,5},{5,4},{6,7},{7,6},{8,9},{9,8},{10,11... | collective-permute-start | bytes 393224 | tf_op jit(solution)/shard_map/ppermute | solution.py:315
  0.5 2.5 %collective-permute-start.1 = (f32[32,2048]{1,0:T(8,128)}, f32[32,2048]{1,0:T(8,128)S(1)}, u32[]{:S(2)}, u32[]{:S(2)}) collective-permute-start(f32[32,2048]{1,0:T(8,128)} %vectors.1), channel_id=1, source_target_pairs={{0,2},{1,3},{2,0},{3,1},{4,6},{5,7},{6,4},{7,5},{8,10},{9,11},{10,... | collective-permute-start | bytes 786440 | tf_op jit(solution)/shard_map/ppermute | solution.py:315
  2.9 2.2 %prepare.1 = (f32[64,128]{1,0:T(8,128)S(1)}, bf16[2,1024,96]{2,1,0:T(8,128)(2,1)S(1)}, bf16[2,64,1024]{2,1,0:T(8,128)(2,1)S(1)}, bf16[2,96,1024]{2,1,0:T(8,128)(2,1)S(1)}, f32[1,2048]{1,0:T(1,128)S(1)}) custom-call(f32[16,2048]{1,0:T(8,128)} %points.1, f32[32,2048]{1,0:T(8,128)} %vectors.1, f32[2,64,1024]{2,1,0:T(8,128)} %refs_5_.1, f32[2,64,64]{2,1,0:T(8,128)} %refs_4_.1, ...), custom_call_target="tpu_custom_call" | custom-call | flops 500000000 | bytes 1500000 | tf_op jit(solution)/shard_map/prepare/pallas_call | solution.py:111
  5.2 0.0 copy-start.4
  5.2 0.1 collective-permute-start.2
  5.3 0.0 copy-start.6
  5.3 0.6 %copy-done.4 = s32[8,6]{1,0:T(8,128)S(1)} copy-done((s32[8,6]{1,0:T(8,128)S(1)}, s32[8,6]{1,0:T(8,128)}, u32[]{:S(2)}) %copy-start.4) | copy-done | bytes 216
  5.9 0.1 copy-done.6
  5.9 5.1 %near_field.4.refs_4_ = f32[2,32,1024]{2,1,0:T(8,128)S(1)} custom-call(s32[8,6]{1,0:T(8,128)S(1)} %copy-done.4, s32[8]{0:T(128)S(1)} %copy-done.6, bf16[2,1024,96]{2,1,0:T(8,128)(2,1)S(1)} %get-tuple-element.23.refs_0_, bf16[2,64,1024]{2,1,0:T(8,128)(2,1)S(1)} %get-tuple-element.24.refs_1_, bf16[2,96,1024]{2,1,0:T(8,128)(2,1)S(1)} %get-tuple-element.26.refs_2_, ...), custom_call_target="tpu_custom_call" | custom-call | flops 500000000 | bytes 1500000 | tf_op jit(solution)/shard_map/near_field/pallas_call | solution.py:233
  11.0 0.0 copy-start.8
  11.1 0.0 collective-permute-done.2
  11.1 0.0 collective-permute-done.3.refs_2_
  11.1 3.6 %collective-permute-start.6 = (f32[2,64,128]{2,1,0:T(8,128)S(1)}, f32[2,64,128]{2,1,0:T(8,128)S(1)}, u32[]{:S(2)}, u32[]{:S(2)}) collective-permute-start(f32[2,64,128]{2,1,0:T(8,128)S(1)} %pad_maximum_fusion.1), channel_id=1, source_target_pairs={{0,12},{4,0},{8,4},{12,8},{1,13},{5,1},{9,5},{13,9},{2,14},{6,2},{... | collective-permute-start | bytes 196616 | tf_op jit(solution)/shard_map/ppermute | solution.py:343
  14.7 0.0 collective-permute-start.5
  14.8 1.0 %collective-permute-start.4 = (f32[2,64,128]{2,1,0:T(8,128)S(1)}, f32[2,64,128]{2,1,0:T(8,128)S(1)}, u32[]{:S(2)}, u32[]{:S(2)}) collective-permute-start(f32[2,64,128]{2,1,0:T(8,128)S(1)} %pad_maximum_fusion.1), channel_id=1, source_target_pairs={{0,4},{4,8},{8,12},{12,0},{1,5},{5,9},{9,13},{13,1},{2,6},{6,10},{... | collective-permute-start | bytes 196616 | tf_op jit(solution)/shard_map/ppermute | solution.py:343
  15.8 2.0 %collective-permute-start = (f32[16,2048]{1,0:T(8,128)S(1)}, f32[16,2048]{1,0:T(8,128)S(1)}, u32[]{:S(2)}, u32[]{:S(2)}) collective-permute-start(f32[16,2048]{1,0:T(8,128)S(1)} %copy-done.8), channel_id=1, source_target_pairs={{0,2},{1,3},{2,0},{3,1},{4,6},{5,7},{6,4},{7,5},{8,10},{9,11},{10,... | collective-permute-start | bytes 393224 | tf_op jit(solution)/shard_map/ppermute | solution.py:315
  17.7 2.1 %near_field.5 = (f32[2,32,1024]{2,1,0:T(8,128)S(1)}, bf16[2,96,1024]{2,1,0:T(8,128)(2,1)S(1)}, f32[1,2048]{1,0:T(1,128)S(1)}) custom-call(s32[8,6]{1,0:T(8,128)S(1)} %copy-done.4, s32[8]{0:T(128)S(1)} %copy-done.6, bf16[2,1024,96]{2,1,0:T(8,128)(2,1)S(1)} %get-tuple-element.23.refs_0_, bf16[2,64,1024]{2,1,0:T(8,128)(2,1)S(1)} %get-tuple-element.24.refs_1_, ...), custom_call_target="tpu_custom_call" | custom-call | flops 500000000 | bytes 1500000 | tf_op jit(solution)/shard_map/near_field/pallas_call | solution.py:233
  19.9 0.0 collective-permute-done.6
  19.9 2.1 %collective-permute-done.5 = f32[2,64,128]{2,1,0:T(8,128)S(1)} collective-permute-done((f32[2,64,128]{2,1,0:T(8,128)S(1)}, f32[2,64,128]{2,1,0:T(8,128)S(1)}, u32[]{:S(2)}, u32[]{:S(2)}) %collective-permute-start.5) | collective-permute-done | bytes 65568 | tf_op jit(solution)/shard_map/ppermute | solution.py:343
  22.0 0.0 collective-permute-done.4
  22.0 0.2 collective-permute-start.8
  22.3 0.0 collective-permute-done.refs_0_
  22.3 0.0 collective-permute-done.1.refs_1_
  22.3 3.8 %near_field.6 = (f32[32,2048]{1,0:T(8,128)S(1)}, bf16[2,1024,96]{2,1,0:T(8,128)(2,1)S(1)}, bf16[2,64,1024]{2,1,0:T(8,128)(2,1)S(1)}) custom-call(s32[8,6]{1,0:T(8,128)S(1)} %copy-done.4, s32[8]{0:T(128)S(1)} %copy-done.6, f32[16,2048]{1,0:T(8,128)S(1)} %collective-permute-done.refs_0_, f32[32,2048]{1,0:T(8,128)S(1)} %collective-permute-done.1.refs_1_, ...), custom_call_target="tpu_custom_call" | custom-call | flops 500000000 | bytes 1500000 | tf_op jit(solution)/shard_map/near_field/pallas_call | solution.py:233
  26.1 0.4 %collective-permute-start.7 = (f32[32,2048]{1,0:T(8,128)S(1)}, f32[32,2048]{1,0:T(8,128)S(1)}, u32[]{:S(2)}, u32[]{:S(2)}) collective-permute-start(f32[32,2048]{1,0:T(8,128)S(1)} %get-tuple-element.37), channel_id=1, source_target_pairs={{0,1},{1,0},{2,3},{3,2},{4,5},{5,4},{6,7},{7,6},{8,9},{9,8},{10,11... | collective-permute-start | bytes 786440 | tf_op jit(solution)/shard_map/ppermute | solution.py:315
  26.5 0.0 copy-start.5
  26.5 0.0 copy-start.7
  26.5 6.6 %near_field.7 = f32[32,2048]{1,0:T(8,128)S(1)} custom-call(s32[8,6]{1,0:T(8,128)S(1)} %copy-done.4, s32[8]{0:T(128)S(1)} %copy-done.6, bf16[2,1024,96]{2,1,0:T(8,128)(2,1)S(1)} %get-tuple-element.34.refs_0_, bf16[2,64,1024]{2,1,0:T(8,128)(2,1)S(1)} %get-tuple-element.35.refs_1_, bf16[2,96,1024]{2,1,0:T(8,128)(2,1)S(1)} %get-tuple-element.26.refs_2_, ...), custom_call_target="tpu_custom_call" | custom-call | flops 500000000 | bytes 1500000 | tf_op jit(solution)/shard_map/near_field/pallas_call | solution.py:233
  33.2 0.0 collective-permute-done.8.refs_1_
  33.2 2.1 %far_field.1 = f32[32,2048]{1,0:T(8,128)S(1)} custom-call(s32[2,8]{1,0:T(2,128)S(1)} %copy-done.5, s32[1,3]{1,0:T(1,128)S(1)} %copy-done.7, f32[4,2,64,128]{3,2,1,0:T(8,128)S(1)} %pad_maximum_fusion.refs_0_, f32[4,2,64,128]{3,2,1,0:T(8,128)S(1)} %collective-permute-done.8.refs_1_, f32[2,16,64]{2,1,0:T(8,128)S(1)} %copy-done.3, f32[4,16,64]{2,1,0:T(8,128)S(1)} %copy-done.2, ...), custom_call_target="tpu_custom_call" | custom-call | flops 500000000 | bytes 1500000 | tf_op jit(solution)/shard_map/far_field/pallas_call | solution.py:302
  35.4 0.0 collective-permute-done.7
  35.4 0.8 %add_add_fusion = f32[32,2048]{1,0:T(8,128)} fusion(f32[32,2048]{1,0:T(8,128)S(1)} %far_field.1, f32[32,2048]{1,0:T(8,128)S(1)} %near_field.7, f32[32,2048]{1,0:T(8,128)S(1)} %collective-permute-done.7), kind=kLoop, calls=%fused_computation.1 | loop fusion | flops 131072 | bytes 1048576 | tf_op jit(solution)/shard_map/add | solution.py:374
  (13 shorter events, 0.0 us)
Async XLA Ops:
  0.0 11.1 %collective-permute-start.3 = (f32[16,2048]{1,0:T(8,128)}, f32[16,2048]{1,0:T(8,128)S(1)}, u32[]{:S(2)}, u32[]{:S(2)}) collective-permute-start(f32[16,2048]{1,0:T(8,128)} %points.1), channel_id=1, source_target_pairs={{0,1},{1,0},{2,3},{3,2},{4,5},{5,4},{6,7},{7,6},{8,9},{9,8},{10,11... | collective-permute-start | bytes 393224 | tf_op jit(solution)/shard_map/ppermute | solution.py:315
  0.5 21.8 %collective-permute-start.1 = (f32[32,2048]{1,0:T(8,128)}, f32[32,2048]{1,0:T(8,128)S(1)}, u32[]{:S(2)}, u32[]{:S(2)}) collective-permute-start(f32[32,2048]{1,0:T(8,128)} %vectors.1), channel_id=1, source_target_pairs={{0,2},{1,3},{2,0},{3,1},{4,6},{5,7},{6,4},{7,5},{8,10},{9,11},{10,... | collective-permute-start | bytes 786440 | tf_op jit(solution)/shard_map/ppermute | solution.py:315
  5.2 0.7 %copy-start.4 = (s32[8,6]{1,0:T(8,128)S(1)}, s32[8,6]{1,0:T(8,128)}, u32[]{:S(2)}) copy-start(s32[8,6]{1,0:T(8,128)} %near_list.7) | copy-start | bytes 580
  5.2 5.9 %collective-permute-start.2 = (f32[64,128]{1,0:T(8,128)S(1)}, f32[64,128]{1,0:T(8,128)S(1)}, u32[]{:S(2)}, u32[]{:S(2)}) collective-permute-start(f32[64,128]{1,0:T(8,128)S(1)} %get-tuple-element.25), channel_id=1, source_target_pairs={{0,2},{1,3},{2,0},{3,1},{4,6},{5,7},{6,4},{7,5},{8,10},{9,11},{10,... | collective-permute-start | bytes 98312 | tf_op jit(solution)/shard_map/ppermute | solution.py:315
  5.3 0.7 %copy-start.6 = (s32[8]{0:T(128)S(1)}, s32[8]{0:T(128)}, u32[]{:S(2)}) copy-start(s32[8]{0:T(128)} %near_count.7) | copy-start | bytes 100
  11.0 4.7 %copy-start.8 = (f32[16,2048]{1,0:T(8,128)S(1)}, f32[16,2048]{1,0:T(8,128)}, u32[]{:S(2)}) copy-start(f32[16,2048]{1,0:T(8,128)} %points.1) | copy-start | bytes 393220
  11.1 8.8 %collective-permute-start.6 = (f32[2,64,128]{2,1,0:T(8,128)S(1)}, f32[2,64,128]{2,1,0:T(8,128)S(1)}, u32[]{:S(2)}, u32[]{:S(2)}) collective-permute-start(f32[2,64,128]{2,1,0:T(8,128)S(1)} %pad_maximum_fusion.1), channel_id=1, source_target_pairs={{0,12},{4,0},{8,4},{12,8},{1,13},{5,1},{9,5},{13,9},{2,14},{6,2},{... | collective-permute-start | bytes 196616 | tf_op jit(solution)/shard_map/ppermute | solution.py:343
  14.7 7.3 %collective-permute-start.5 = (f32[2,64,128]{2,1,0:T(8,128)S(1)}, f32[2,64,128]{2,1,0:T(8,128)S(1)}, u32[]{:S(2)}, u32[]{:S(2)}) collective-permute-start(f32[2,64,128]{2,1,0:T(8,128)S(1)} %pad_maximum_fusion.1), channel_id=1, source_target_pairs={{0,8},{4,12},{8,0},{12,4},{1,9},{5,13},{9,1},{13,5},{2,10},{6,14},... | collective-permute-start | bytes 196616 | tf_op jit(solution)/shard_map/ppermute | solution.py:343
  14.8 7.3 %collective-permute-start.4 = (f32[2,64,128]{2,1,0:T(8,128)S(1)}, f32[2,64,128]{2,1,0:T(8,128)S(1)}, u32[]{:S(2)}, u32[]{:S(2)}) collective-permute-start(f32[2,64,128]{2,1,0:T(8,128)S(1)} %pad_maximum_fusion.1), channel_id=1, source_target_pairs={{0,4},{4,8},{8,12},{12,0},{1,5},{5,9},{9,13},{13,1},{2,6},{6,10},{... | collective-permute-start | bytes 196616 | tf_op jit(solution)/shard_map/ppermute | solution.py:343
  15.8 6.5 %collective-permute-start = (f32[16,2048]{1,0:T(8,128)S(1)}, f32[16,2048]{1,0:T(8,128)S(1)}, u32[]{:S(2)}, u32[]{:S(2)}) collective-permute-start(f32[16,2048]{1,0:T(8,128)S(1)} %copy-done.8), channel_id=1, source_target_pairs={{0,2},{1,3},{2,0},{3,1},{4,6},{5,7},{6,4},{7,5},{8,10},{9,11},{10,... | collective-permute-start | bytes 393224 | tf_op jit(solution)/shard_map/ppermute | solution.py:315
  22.0 11.1 %collective-permute-start.8 = (f32[4,2,64,128]{3,2,1,0:T(8,128)S(1)}, f32[4,2,64,128]{3,2,1,0:T(8,128)S(1)}, u32[]{:S(2)}, u32[]{:S(2)}) collective-permute-start(f32[4,2,64,128]{3,2,1,0:T(8,128)S(1)} %pad_maximum_fusion.refs_0_), channel_id=1, source_target_pairs={{0,1},{1,0},{2,3},{3,2},{4,5},{5,4},{6,7},{7,6},{8,9},{9,8},{10,11... | collective-permute-start | bytes 786440 | tf_op jit(solution)/shard_map/ppermute | solution.py:315
  26.1 9.3 %collective-permute-start.7 = (f32[32,2048]{1,0:T(8,128)S(1)}, f32[32,2048]{1,0:T(8,128)S(1)}, u32[]{:S(2)}, u32[]{:S(2)}) collective-permute-start(f32[32,2048]{1,0:T(8,128)S(1)} %get-tuple-element.37), channel_id=1, source_target_pairs={{0,1},{1,0},{2,3},{3,2},{4,5},{5,4},{6,7},{7,6},{8,9},{9,8},{10,11... | collective-permute-start | bytes 786440 | tf_op jit(solution)/shard_map/ppermute | solution.py:315
  26.5 6.7 %copy-start = (f32[2,64,1024]{2,1,0:T(8,128)S(1)}, f32[2,64,1024]{2,1,0:T(8,128)}, u32[]{:S(2)}) copy-start(f32[2,64,1024]{2,1,0:T(8,128)} %refs_5_.1) | copy-start | bytes 1572868
  26.5 6.7 %copy-start.1 = (f32[2,64,64]{2,1,0:T(8,128)S(1)}, f32[2,64,64]{2,1,0:T(8,128)}, u32[]{:S(2)}) copy-start(f32[2,64,64]{2,1,0:T(8,128)} %refs_4_.1) | copy-start | bytes 98308
  26.5 6.7 %copy-start.2 = (f32[4,16,64]{2,1,0:T(8,128)S(1)}, f32[4,16,64]{2,1,0:T(8,128)}, u32[]{:S(2)}) copy-start(f32[4,16,64]{2,1,0:T(8,128)} %refs_3_.1) | copy-start | bytes 49156
  26.5 6.7 %copy-start.3 = (f32[2,16,64]{2,1,0:T(8,128)S(1)}, f32[2,16,64]{2,1,0:T(8,128)}, u32[]{:S(2)}) copy-start(f32[2,16,64]{2,1,0:T(8,128)} %refs_2_.1) | copy-start | bytes 24580
  26.5 6.7 %copy-start.5 = (s32[2,8]{1,0:T(2,128)S(1)}, s32[2,8]{1,0:T(2,128)}, u32[]{:S(2)}) copy-start(s32[2,8]{1,0:T(2,128)} %far_list.1) | copy-start | bytes 196
  26.5 6.7 %copy-start.7 = (s32[1,3]{1,0:T(1,128)S(1)}, s32[1,3]{1,0:T(1,128)}, u32[]{:S(2)}) copy-start(s32[1,3]{1,0:T(1,128)} %parent_far.1) | copy-start | bytes 40
